TPU v7x, 256 devices: a whole 4x4x8 slice. The times are simulated.
256 devices in a mesh: prow: 16 (over x, y), pcol: 16 (over z, core).
Axes of the slice: x: 4, y: 4, z: 8, core: 2. Of those that a mesh axis runs over, the one named last changes fastest.
Arguments:
- inverse_tiles: float32 [24576, 24576], P('prow', 'pcol'), may hold values from -6 to 6
- factor_rows: float32 [24576, 512], P('prow'), may hold values from -0.0390625 to 0.0390625
- diag_inverse: float32 [512, 512], P('prow', 'pcol'), may hold values from -6 to 6
- pattern: int32 [192], replicated, may hold values from 0 to 1, as said below
Outputs:
- column_block: float32 [24576, 512], P(('prow', 'pcol'))
- diagonal_block: float32 [512, 512], P('prow', 'pcol')
Inputs may be any that keep to these rules, and one draw needn't show every extreme that they name: `pattern`: 1 where the block of ancestor rows lies in the supernode's structure, else 0; the first block always lies in it and the last never.
All inputs are finite; a program needn't handle non-finite values.
Results may differ from a plain program's by a relative error of at most 0.000078.
Values sent between devices are 32-bit elements; how exact they have to be, the bound alone decides.
A program may use at most 64 MiB of HBM per device.

v0:
```python
import jax
import jax.numpy as jnp
from jax import lax
from jax.sharding import PartitionSpec as P

BLK = 128


def broadcast(shard, axis, root):
    mine = lax.axis_index(axis) == root
    return lax.psum(jnp.where(mine, shard, jnp.zeros_like(shard)), axis)


def row_select(pattern, first_row, row_count):
    global_rows = first_row + lax.iota(jnp.int32, row_count)
    block_ids = global_rows // BLK
    blocks = lax.iota(jnp.int32, pattern.shape[0])
    match = block_ids[:, None] == blocks[None, :]
    return jnp.sum(jnp.where(match, pattern[None, :], 0), axis=1).astype(jnp.float32)


def local(inverse_tiles, factor_rows, diag_inverse, pattern):
    n_row = lax.axis_size("prow")
    n_col = lax.axis_size("pcol")
    row_index = lax.axis_index("prow")
    col_index = lax.axis_index("pcol")
    tile_rows = inverse_tiles.shape[0]
    width = factor_rows.shape[1]
    col_ratio = n_col // n_row
    tile_mask = row_select(pattern, row_index * tile_rows, tile_rows)
    masked_rows = factor_rows * tile_mask[:, None]
    root_index = col_index // col_ratio
    column_factor = broadcast(masked_rows, "prow", root_index)
    out_rows = tile_rows // n_col
    own_mask = lax.dynamic_slice_in_dim(tile_mask, col_index * out_rows, out_rows, 0)
    summed = lax.psum_scatter(
        jnp.dot(
            inverse_tiles,
            column_factor,
            precision=lax.Precision.HIGHEST,
            preferred_element_type=jnp.float32,
        ),
        "pcol",
        scatter_dimension=0,
        tiled=True,
    )
    column_block = -summed * own_mask[:, None]
    own_factor = lax.dynamic_slice_in_dim(masked_rows, col_index * out_rows, out_rows, 0)
    correction = jnp.dot(
        own_factor.T,
        column_block,
        precision=lax.Precision.HIGHEST,
        preferred_element_type=jnp.float32,
    )
    share_rows = width // n_row
    share_cols = width // n_col
    total = lax.psum(correction, ("prow", "pcol"))
    mine = lax.dynamic_slice_in_dim(total, row_index * share_rows, share_rows, 0)
    mine = lax.dynamic_slice_in_dim(mine, col_index * share_cols, share_cols, 1)
    diagonal_block = diag_inverse - mine
    return (column_block, diagonal_block)


def solution(mesh):
    return jax.shard_map(
        local,
        mesh=mesh,
        in_specs=(P("prow", "pcol"), P("prow", None), P("prow", "pcol"), P()),
        out_specs=(P(("prow", "pcol"), None), P("prow", "pcol")),
        check_vma=False,
    )
```

profile of v0, /device:TPU:2, one launch (start us, length us, event | category | flops | bytes accessed | tf_op | source)
XLA Modules:
  0.0 486.7 jit_solution(2618782349382456584)
XLA Ops:
  7.2 0.0 all-reduce.3.cloned.1.call-start
  7.2 0.9 select_reduce_fusion
  8.2 4.1 broadcast_select_fusion
  12.2 0.0 all-reduce.3.cloned.1.call-update
  12.3 0.0 reduce-scatter.4.cloned.1.call-start
  12.3 108.1 %all-reduce.3.cloned.1.call-done = f32[1536,512]{1,0:T(8,128)} async-done(((f32[1536,512]{1,0:T(8,128)}), f32[1536,512]{1,0:T(8,128)}) %all-reduce.3.cloned.1.call-update) | async-done | bytes 3145744 | tf_op jit(solution)/shard_map/psum | solution.py:11
  120.4 33.8 %convolution_bitcast_fusion = f32[1536,512]{0,1:T(8,128)} fusion(f32[1536,512]{1,0:T(8,128)} %all-reduce.3.cloned.1.call-done, f32[1536,1536]{1,0:T(8,128)} %param.4), kind=kOutput, calls=%fused_computation | convolution fusion | flops 14495514624 | bytes 15728640 | tf_op jit(solution)/shard_map/dot_general | solution.py:37
  154.1 3.5 copy.9
  157.7 0.0 copy-start
  157.7 0.0 reduce-scatter.4.cloned.1.call-update
  157.7 0.0 all-reduce.5.cloned.1.call-start
  157.8 0.1 dynamic_slice.10
  157.9 61.0 %reduce-scatter.4.cloned.1.call-done = f32[96,512]{1,0:T(8,128)} async-done(((f32[1536,512]{1,0:T(8,128)}), f32[96,512]{1,0:T(8,128)}) %reduce-scatter.4.cloned.1.call-update) | async-done | bytes 196624
  218.8 1.8 copy.10
  220.6 1.0 negate_multiply_fusion
  221.6 2.1 fusion
  223.6 0.0 all-reduce.5.cloned.1.call-update
  223.7 0.8 copy.8
  224.5 254.3 %all-reduce.5.cloned.1.call-done = f32[512,512]{1,0:T(8,128)} async-done(((f32[512,512]{1,0:T(8,128)}), f32[512,512]{1,0:T(8,128)}) %all-reduce.5.cloned.1.call-update) | async-done | bytes 1048592 | tf_op jit(solution)/shard_map/psum | solution.py:57
  478.8 0.0 copy-done
  478.8 1.5 dynamic-slice_subtract_fusion
  (2 shorter events, 0.0 us)
Async XLA Ops:
  7.2 113.2 %all-reduce.3.cloned.1.call-start = ((), (), s32[]{:S(2)}) async-start(), calls=%async_computation.1 | async-start | bytes 6291456 | tf_op jit(solution)/shard_map/psum | solution.py:11
  12.3 206.6 %reduce-scatter.4.cloned.1.call-start = ((), (), s32[]{:S(2)}) async-start(), calls=%async_computation.3 | async-start | bytes 3342336
  157.7 321.1 %copy-start = (f32[32,32]{1,0:T(8,128)S(1)}, f32[32,32]{1,0:T(8,128)}, u32[]{:S(2)}) copy-start(f32[32,32]{1,0:T(8,128)} %param.6) | copy-start | bytes 12292
  157.7 321.0 %all-reduce.5.cloned.1.call-start = ((), (), s32[]{:S(2)}) async-start(), calls=%async_computation.2 | async-start | bytes 2097152 | tf_op jit(solution)/shard_map/psum | solution.py:57
Sparse Core Ops, SparseCore 0:
  12.4 107.9 all-reduce.2
  157.8 60.9 reduce-scatter.3
  224.3 254.4 all-reduce.4
where the time goes:
time: 487 us
  waiting for transfers between devices  423 us (87%)
  matrix products  35.8 us (7%)
  between operations  13.8 us (3%)
  other arithmetic  7.43 us (2%)
  local copies, waits for them, and re-layouts  6.18 us (1%)
    psum x1, waiting for transfers between devices, local(): total = lax.psum(correction, ('prow', 'pcol'))  254 us
    psum x1, waiting for transfers between devices, broadcast(): return lax.psum(jnp.where(mine, shard, jnp.zeros_like(shard)), axis)  108 us
    unnamed x4, waiting for transfers between devices  61 us
    dot_general x1, matrix products, local(): jnp.dot(inverse_tiles, column_factor, precision=lax.Precision.HIGHEST, pr...  33.8 us
  transfers between devices with their start and end apart: 3, of which 3 were waited for; matrix products, arithmetic and copies ran while one was open for 0% of the time, Pallas kernels for 0%

commit v1 on v0

--- a/solution.py
+++ b/solution.py
@@ -54,7 +54,9 @@
     )
     share_rows = width // n_row
     share_cols = width // n_col
-    total = lax.psum(correction, ("prow", "pcol"))
+    total = correction
+    for over in ("prow", "pcol"):
+        total = lax.psum(total, over)
     mine = lax.dynamic_slice_in_dim(total, row_index * share_rows, share_rows, 0)
     mine = lax.dynamic_slice_in_dim(mine, col_index * share_cols, share_cols, 1)
     diagonal_block = diag_inverse - mine

time: 487 us -> 441 us (0.906)
  waiting for transfers between devices: 423 us -> 377 us
    psum x1 -> x2, waiting for transfers between devices: 254 us -> 208 us  [local(): total = lax.psum(total, over)]
    unnamed x4 -> x5, waiting for transfers between devices: 61 us -> 61 us
  transfers between devices with their start and end apart: 3 -> 4, of which waited for: 3 -> 4; matrix products, arithmetic and copies ran while one was open for 0% -> 0% of each run, Pallas kernels for 0% -> 0%
where the time goes in v1:
time: 441 us; the launch traced here: 440 us
  waiting for transfers between devices  377 us (85%)
  matrix products  35.8 us (8%)
  between operations  13.8 us (3%)
  other arithmetic  7.43 us (2%)
  local copies, waits for them, and re-layouts  6.19 us (1%)
    psum x2, waiting for transfers between devices, local(): total = lax.psum(total, over)  208 us
    psum x1, waiting for transfers between devices, broadcast(): return lax.psum(jnp.where(mine, shard, jnp.zeros_like(shard)), axis)  108 us
    unnamed x5, waiting for transfers between devices  61 us
    dot_general x1, matrix products, local(): jnp.dot(inverse_tiles, column_factor, precision=lax.Precision.HIGHEST, pr...  33.8 us
  transfers between devices with their start and end apart: 4, of which 4 were waited for; matrix products, arithmetic and copies ran while one was open for 0% of the time, Pallas kernels for 0%

profile of v1, /device:TPU:2, one launch (start us, length us, event | category | flops | bytes accessed | tf_op | source)
XLA Modules:
  0.0 440.4 jit_solution(15949288918015220223)
XLA Ops:
  7.2 0.0 all-reduce.4.cloned.1.call-start
  7.2 0.9 select_reduce_fusion
  8.2 4.1 broadcast_select_fusion
  12.2 0.0 all-reduce.4.cloned.1.call-update
  12.3 0.0 reduce-scatter.4.cloned.1.call-start
  12.3 108.1 %all-reduce.4.cloned.1.call-done = f32[1536,512]{1,0:T(8,128)} async-done(((f32[1536,512]{1,0:T(8,128)}), f32[1536,512]{1,0:T(8,128)}) %all-reduce.4.cloned.1.call-update) | async-done | bytes 3145744 | tf_op jit(solution)/shard_map/psum | solution.py:11
  120.4 33.8 %convolution_bitcast_fusion = f32[1536,512]{0,1:T(8,128)} fusion(f32[1536,512]{1,0:T(8,128)} %all-reduce.4.cloned.1.call-done, f32[1536,1536]{1,0:T(8,128)} %param.4), kind=kOutput, calls=%fused_computation | convolution fusion | flops 14495514624 | bytes 15728640 | tf_op jit(solution)/shard_map/dot_general | solution.py:37
  154.1 3.5 copy.9
  157.7 0.0 reduce-scatter.4.cloned.1.call-update
  157.7 0.0 copy-start
  157.7 0.0 all-reduce.6.cloned.1.call-start
  157.8 0.1 dynamic_slice.10
  157.9 61.0 %reduce-scatter.4.cloned.1.call-done = f32[96,512]{1,0:T(8,128)} async-done(((f32[1536,512]{1,0:T(8,128)}), f32[96,512]{1,0:T(8,128)}) %reduce-scatter.4.cloned.1.call-update) | async-done | bytes 196624
  218.8 1.8 copy.10
  220.6 1.0 negate_multiply_fusion
  221.6 2.1 fusion
  223.6 0.0 all-reduce.6.cloned.1.call-update
  223.7 0.0 all-reduce.8.cloned.1.call-start
  223.7 95.4 %all-reduce.6.cloned.1.call-done = f32[512,512]{1,0:T(8,128)} async-done(((f32[512,512]{1,0:T(8,128)}), f32[512,512]{1,0:T(8,128)}) %all-reduce.6.cloned.1.call-update) | async-done | bytes 1048592 | tf_op jit(solution)/shard_map/psum | solution.py:59
  319.1 0.0 all-reduce.8.cloned.1.call-update
  319.1 0.8 copy.8
  319.9 112.5 %all-reduce.8.cloned.1.call-done = f32[512,512]{1,0:T(8,128)} async-done(((f32[512,512]{1,0:T(8,128)}), f32[512,512]{1,0:T(8,128)}) %all-reduce.8.cloned.1.call-update) | async-done | bytes 1048592 | tf_op jit(solution)/shard_map/psum | solution.py:59
  432.4 0.0 copy-done
  432.4 1.5 dynamic-slice_subtract_fusion
  (2 shorter events, 0.0 us)
Async XLA Ops:
  7.2 113.2 %all-reduce.4.cloned.1.call-start = ((), (), s32[]{:S(2)}) async-start(), calls=%async_computation.1 | async-start | bytes 6291456 | tf_op jit(solution)/shard_map/psum | solution.py:11
  12.3 206.6 %reduce-scatter.4.cloned.1.call-start = ((), (), s32[]{:S(2)}) async-start(), calls=%async_computation.4 | async-start | bytes 3342336
  157.7 274.6 %copy-start = (f32[32,32]{1,0:T(8,128)S(1)}, f32[32,32]{1,0:T(8,128)}, u32[]{:S(2)}) copy-start(f32[32,32]{1,0:T(8,128)} %param.6) | copy-start | bytes 12292
  157.7 161.3 %all-reduce.6.cloned.1.call-start = ((), (), s32[]{:S(2)}) async-start(), calls=%async_computation.2 | async-start | bytes 2097152 | tf_op jit(solution)/shard_map/psum | solution.py:59
  223.7 208.7 %all-reduce.8.cloned.1.call-start = ((), (), s32[]{:S(2)}) async-start(), calls=%async_computation.3 | async-start | bytes 2097152 | tf_op jit(solution)/shard_map/psum | solution.py:59
Sparse Core Ops, SparseCore 0:
  12.4 107.9 all-reduce.3
  157.8 60.9 reduce-scatter.3
  223.8 95.2 all-reduce.5
  321.2 111.0 all-reduce.7
